TPU v7x, 256 devices: a whole 4x4x8 slice. The times are simulated.
256 devices in a mesh: seq: 32 (over y, z_lo, core), dp: 8 (over x, z_hi).
Axes of the slice: x: 4, y: 4, z: 8 (z_hi: 2, z_lo: 4; z = z_hi * 4 + z_lo), core: 2. Of those that a mesh axis runs over, the one named last changes fastest.
Arguments:
- queries: bfloat16 [131072, 768], P(('dp', 'seq')), parts along dimension 0, may hold values from -400 to 400
- keys: bfloat16 [131072, 768], P(('dp', 'seq')), parts along dimension 0, may hold values from -16 to 16
- values: bfloat16 [131072, 768], P(('dp', 'seq')), parts along dimension 0, may hold values from -6 to 6
- offsets: int32 [5, 16], replicated, may hold values from 0 to 15, as said below
- out_weight: bfloat16 [768, 768], replicated, may hold values from -0.21875 to 0.21875
Outputs:
- projected: bfloat16 [131072, 768], P(('dp', 'seq')), parts along dimension 0
There are 8 independent parts, one for each index of `dp`. A program takes and returns all parts, laid end to end along the dimension named above; an argument that names none is the same for every part. Nothing has to cross between parts.
Inputs may be any that keep to these rules, and one draw needn't show every extreme that they name: offsets[l, h] lies in 0 to 2**l - 1; at a level l with 2**l <= 16, each value 0 to 2**l - 1 is taken by exactly 16 / 2**l heads; at a level with 2**l > 16, the heads take the distinct values 0 to 15.
All inputs are finite; a program needn't handle non-finite values.
Results may differ from a plain program's by a relative error of at most 0.0055.
Values may be sent and summed in bfloat16 or wider, within the bound.
A program may use at most 128 MiB of HBM per device.

v0:
```python
import math

import jax
import jax.numpy as jnp
from jax import lax
from jax.experimental import pallas as pl
from jax.experimental.pallas import tpu as pltpu
from jax.sharding import PartitionSpec as P

MESH = pl.DeviceIdType.MESH
BF = jnp.bfloat16
F32 = jnp.float32
ROWS = 512
WIDTH = 768
HALF = 384
HD = 48
NH = 8
COEF = math.log2(math.e) / math.sqrt(HD)
NT = (((1,), (1,)), ((), ()))
KEPT = [ROWS >> level for level in range(5)]


def reversed_bits(x, bits):
    out = jnp.zeros_like(x)
    for b in range(bits):
        out = out + ((x >> b) & 1) * (1 << (bits - 1 - b))
    return out


def window(first, count):
    lo, hi = HD * first, HD * (first + count)
    start = lo // 128 * 128
    width = 128 if hi <= start + 128 else 256
    return start, width


def head_mask(head, start, width):
    lane = lax.broadcasted_iota(jnp.int32, (1, width), 1) + start
    return (lane >= HD * head) & (lane < HD * head + HD)


def softmax_unit(q, k, v):
    s = lax.dot_general(q, k, NT, preferred_element_type=F32)
    top = jnp.max(s, axis=1, keepdims=True) * COEF
    p = jnp.exp2(s * COEF - top)
    total = jnp.sum(p, axis=1, keepdims=True)
    o = jnp.dot(p.astype(BF), v, preferred_element_type=F32)
    return o, top, total


def kernel(
    off_ref, q_ref, k_ref, v_ref, w_ref, out_ref,
    stage, halves, s1, s2, s3, c4, r2, r3, y4, q1, q2, q3, q4,
    acc0, acc1, acc2, acc3, acc4, top0, top1, top2, top3, top4,
    sum0, sum1, sum2, sum3, sum4, unperm, msend, mrecv, send_sem, recv_sem,
):
    me = lax.axis_index("seq")
    core = lax.rem(me, 2)
    z = lax.rem(me // 2, 4)
    y = me // 8

    def at(yy, zz, cc):
        return {"seq": (yy * 4 + zz) * 2 + cc}

    sibling = at(y, z, 1 - core)
    z_peers = [at(y, z + 1 - 2 * lax.rem(z, 2), core), at(y, lax.rem(z + 2, 4), core), at(y, 3 - z, core)]
    y_peers = [at(lax.rem(y + d, 4), z, core) for d in (1, 2, 3)]
    barrier = pltpu.get_barrier_semaphore()
    for peer in [sibling] + z_peers + y_peers:
        pl.semaphore_signal(barrier, inc=1, device_id=peer, device_id_type=MESH)

    def remote(slot, src, dst, peer):
        return pltpu.make_async_remote_copy(
            src_ref=src, dst_ref=dst, send_sem=send_sem.at[slot], recv_sem=recv_sem.at[slot],
            device_id=peer, device_id_type=MESH,
        )

    dest = lax.broadcasted_iota(jnp.int32, (ROWS, 1), 0)
    source = (dest & 31) * 16 + reversed_bits(dest >> 5, 4)
    lane512 = lax.broadcasted_iota(jnp.int32, (ROWS, ROWS), 1)
    perm = jnp.where(lane512 == source, 1.0, 0.0).astype(BF)
    mine = pl.ds(pl.multiple_of(core * HALF, 128), HALF)
    theirs = pl.ds(pl.multiple_of((1 - core) * HALF, 128), HALF)

    def permuted(ref, lanes):
        return jnp.dot(perm, ref[:, lanes], preferred_element_type=F32).astype(BF)

    stage[0] = permuted(k_ref, theirs)
    stage[1] = permuted(v_ref, theirs)
    pl.semaphore_wait(barrier, 7)
    kv_copy = remote(0, stage.at[pl.ds(0, 2)], halves.at[1, pl.ds(0, 2)], sibling)
    kv_copy.start()
    stage[2] = permuted(q_ref, theirs)
    q_copy = remote(1, stage.at[2], halves.at[1, 2], sibling)
    q_copy.start()
    halves[0, 0] = permuted(k_ref, mine)
    halves[0, 1] = permuted(v_ref, mine)

    offs = off_ref[...].astype(BF)
    head_row = lax.broadcasted_iota(jnp.int32, (16, HALF), 0)
    head_col = lax.broadcasted_iota(jnp.int32, (16, HALF), 1) // HD + NH * core
    off_cols = jnp.dot(offs, jnp.where(head_row == head_col, 1.0, 0.0).astype(BF), preferred_element_type=F32)
    stat_row = lax.broadcasted_iota(jnp.int32, (16, 128), 0)
    stat_col = (lax.broadcasted_iota(jnp.int32, (16, 128), 1) & 7) + NH * core
    off_stat = jnp.dot(offs, jnp.where(stat_row == stat_col, 1.0, 0.0).astype(BF), preferred_element_type=F32)
    block_cols, block_stat = [None], [None]
    for level in range(1, 5):
        block_cols.append(reversed_bits(off_cols[level:level + 1].astype(jnp.int32), level))
        block_stat.append(reversed_bits(off_stat[level:level + 1].astype(jnp.int32), level))

    def select(src, kind, level):
        n = KEPT[level]
        kept = halves[src, kind, 0:n]
        for b in range(1, 1 << level):
            kept = jnp.where(block_cols[level] == b, halves[src, kind, b * n:(b + 1) * n], kept)
        return kept

    c4_own = c4.at[0]
    for kind in range(2):
        c4[0, kind, 0:KEPT[4]] = select(0, kind, 4)
        s3[kind, 0:KEPT[3]] = select(0, kind, 3)
        s2[kind, 0:KEPT[2]] = select(0, kind, 2)
        s1[kind, 0:KEPT[1]] = select(0, kind, 1)
    kv_copy.wait_recv()
    for kind in range(2):
        c4[0, kind, KEPT[4]:] = select(1, kind, 4)
    z4 = [remote(2 + i, c4_own, c4.at[1 + i], z_peers[i]) for i in range(3)]
    for c in z4:
        c.start()
    for kind in range(2):
        s3[kind, KEPT[3]:] = select(1, kind, 3)
        s2[kind, KEPT[2]:] = select(1, kind, 2)
    z3 = [remote(5 + i, s3, r3.at[i], z_peers[i]) for i in range(3)]
    z2 = remote(8, s2, r2, z_peers[0])
    for kind in range(2):
        s1[kind, KEPT[1]:] = select(1, kind, 1)
    halves[0, 2] = permuted(q_ref, mine)
    q_copy.wait_recv()
    for src in range(2):
        q4[src * KEPT[4]:(src + 1) * KEPT[4]] = select(src, 2, 4)
        q3[src * KEPT[3]:(src + 1) * KEPT[3]] = select(src, 2, 3)
        q2[src * KEPT[2]:(src + 1) * KEPT[2]] = select(src, 2, 2)
        q1[src * KEPT[1]:(src + 1) * KEPT[1]] = select(src, 2, 1)

    stat_lane = lax.broadcasted_iota(jnp.int32, (1, 128), 1) & 7

    def attend(q_of, k_of, v_of, group, rows, acc, top_ref, sum_ref):
        tops = jnp.zeros((rows, 128), F32)
        sums = jnp.zeros((rows, 128), F32)
        written = set()
        for first in range(0, NH, group):
            start, width = window(first, group)
            masks = [head_mask(first + g, start, width) for g in range(group)]
            q = q_of(start, width)
            if group == 1:
                stack = q
                k = jnp.where(masks[0], k_of(start, width), jnp.zeros((), BF))
            else:
                stack = jnp.concatenate([jnp.where(m, q, jnp.zeros((), BF)) for m in masks], axis=0)
                k = k_of(start, width)
            o, top, total = softmax_unit(stack, k, v_of(start, width))
            for t in range(start, start + width, 128):
                part = None
                for g in range(group):
                    lo, hi = HD * (first + g), HD * (first + g + 1)
                    if hi <= t or lo >= t + 128:
                        continue
                    piece = o[g * rows:(g + 1) * rows, t - start:t - start + 128]
                    mask = masks[g][:, t - start:t - start + 128]
                    if part is None:
                        part = jnp.where(mask, piece, acc[:, t:t + 128]) if t in written else piece
                    else:
                        part = jnp.where(mask, piece, part)
                acc[:, t:t + 128] = part
                written.add(t)
            for g in range(group):
                lanes = stat_lane == first + g
                tops = jnp.where(lanes, top[g * rows:(g + 1) * rows], tops)
                sums = jnp.where(lanes, total[g * rows:(g + 1) * rows], sums)
        top_ref[...] = tops
        sum_ref[...] = sums

    def level0(s, carry):
        attend(
            lambda a, w: halves[s, 2, :, a:a + w],
            lambda a, w: halves[s, 0, :, a:a + w],
            lambda a, w: halves[s, 1, :, a:a + w],
            1, ROWS, acc0.at[s], top0.at[s], sum0.at[s],
        )
        return carry

    level0(0, 0)
    for c in z4:
        c.wait_recv()
    y4c = [remote(9 + i, c4, y4.at[i], y_peers[i]) for i in range(3)]
    for c in y4c:
        c.start()
    for c in z3:
        c.start()
    z2.start()
    level0(1, 0)
    attend(
        lambda a, w: q1[:, a:a + w], lambda a, w: s1[0, :, a:a + w], lambda a, w: s1[1, :, a:a + w],
        1, 2 * KEPT[1], acc1, top1, sum1,
    )
    dest2 = lax.broadcasted_iota(jnp.int32, (ROWS, 1), 0)
    back = reversed_bits(dest2 & 15, 4) * 32 + (dest2 >> 4)
    unperm[...] = jnp.where(lane512 == back, 1.0, 0.0).astype(BF)
    z2.wait_recv()

    def both2(kind):
        return lambda a, w: jnp.concatenate([s2[kind, :, a:a + w], r2[kind, :, a:a + w]], axis=0)

    attend(lambda a, w: q2[:, a:a + w], both2(0), both2(1), 2, 2 * KEPT[2], acc2, top2, sum2)
    for c in z3:
        c.wait_recv()

    def all3(kind):
        return lambda a, w: jnp.concatenate([s3[kind, :, a:a + w]] + [r3[i, kind, :, a:a + w] for i in range(3)], axis=0)

    attend(lambda a, w: q3[:, a:a + w], all3(0), all3(1), 4, 2 * KEPT[3], acc3, top3, sum3)
    for c in y4c:
        c.wait_recv()

    def all4(kind):
        return lambda a, w: jnp.concatenate(
            [c4[b, kind, :, a:a + w] for b in range(4)]
            + [y4[i, b, kind, :, a:a + w] for i in range(3) for b in range(4)], axis=0)

    attend(lambda a, w: q4[:, a:a + w], all4(0), all4(1), 4, 2 * KEPT[4], acc4, top4, sum4)

    spread_row = lax.broadcasted_iota(jnp.int32, (128, HALF), 0)
    spread_col = lax.broadcasted_iota(jnp.int32, (128, HALF), 1) // HD
    spread = jnp.where((spread_row < 16) & ((spread_row & 7) == spread_col), 1.0, 0.0).astype(BF)
    is_high = lax.broadcasted_iota(jnp.int32, (1, 128), 1) < 8
    row_class = lax.broadcasted_iota(jnp.int32, (ROWS, 1), 0) >> 5
    accs = [acc0, acc1, acc2, acc3, acc4]
    tops = [top0, top1, top2, top3, top4]
    sums = [sum0, sum1, sum2, sum3, sum4]

    def merge(s):
        def full(refs, level):
            if level == 0:
                return refs[0][s]
            n = KEPT[level]
            part = refs[level][s * n:(s + 1) * n]
            return jnp.concatenate([part] * (1 << level), axis=0)

        level_tops = [full(tops, 0)]
        for level in range(1, 5):
            match = (row_class >> (4 - level)) == block_stat[level]
            level_tops.append(jnp.where(match, full(tops, level), -1e30))
        peak = level_tops[0]
        for t in level_tops[1:]:
            peak = jnp.maximum(peak, t)
        shares = [jnp.exp2(t - peak) for t in level_tops]
        den = shares[0] * full(sums, 0)
        for level in range(1, 5):
            den = den + shares[level] * full(sums, level)
        inv = 1.0 / den
        merged = None
        for level in range(5):
            weight = shares[level] * inv
            high = weight.astype(BF).astype(F32)
            packed = jnp.where(is_high, high, weight - high).astype(BF)
            wide = jnp.dot(packed, spread, preferred_element_type=F32)
            term = wide * full(accs, level)
            merged = term if merged is None else merged + term
        return jnp.dot(unperm[...], merged.astype(BF), preferred_element_type=F32).astype(BF)

    msend[...] = merge(1)
    m_copy = remote(12, msend, mrecv, sibling)
    m_copy.start()
    own = merge(0)
    w_mine = w_ref[pl.ds(pl.multiple_of(core * HALF, 128), HALF), :]
    w_theirs = w_ref[pl.ds(pl.multiple_of((1 - core) * HALF, 128), HALF), :]
    projected = jnp.dot(own, w_mine, preferred_element_type=F32)
    m_copy.wait_recv()
    projected = projected + jnp.dot(mrecv[...], w_theirs, preferred_element_type=F32)
    out_ref[...] = projected.astype(BF)
    for c in [kv_copy, q_copy] + z4 + z3 + [z2] + y4c + [m_copy]:
        c.wait_send()


def body(queries, keys, values, offsets, out_weight):
    vmem = pl.BlockSpec(memory_space=pltpu.VMEM)
    n = KEPT
    scratch = [
        pltpu.VMEM((3, ROWS, HALF), BF),
        pltpu.VMEM((2, 3, ROWS, HALF), BF),
        pltpu.VMEM((2, 2 * n[1], HALF), BF),
        pltpu.VMEM((2, 2 * n[2], HALF), BF),
        pltpu.VMEM((2, 2 * n[3], HALF), BF),
        pltpu.VMEM((4, 2, 2 * n[4], HALF), BF),
        pltpu.VMEM((2, 2 * n[2], HALF), BF),
        pltpu.VMEM((3, 2, 2 * n[3], HALF), BF),
        pltpu.VMEM((3, 4, 2, 2 * n[4], HALF), BF),
    ]
    scratch += [pltpu.VMEM((2 * n[level], HALF), BF) for level in range(1, 5)]
    scratch += [pltpu.VMEM((2, ROWS, HALF), F32)]
    scratch += [pltpu.VMEM((2 * n[level], HALF), F32) for level in range(1, 5)]
    for _ in range(2):
        scratch += [pltpu.VMEM((2, ROWS, 128), F32)]
        scratch += [pltpu.VMEM((2 * n[level], 128), F32) for level in range(1, 5)]
    scratch += [
        pltpu.VMEM((ROWS, ROWS), BF),
        pltpu.VMEM((ROWS, HALF), BF),
        pltpu.VMEM((ROWS, HALF), BF),
        pltpu.SemaphoreType.DMA((13,)),
        pltpu.SemaphoreType.DMA((13,)),
    ]
    return pl.pallas_call(
        kernel,
        out_shape=jax.ShapeDtypeStruct((ROWS, WIDTH), BF),
        in_specs=[vmem] * 5,
        out_specs=vmem,
        scratch_shapes=scratch,
        compiler_params=pltpu.CompilerParams(collective_id=0, has_side_effects=True, vmem_limit_bytes=56 << 20),
        cost_estimate=pl.CostEstimate(flops=3 * 10**9, bytes_accessed=5 * 10**6, transcendentals=9 * 10**6),
        name="dilated_attention",
    )(offsets, queries, keys, values, out_weight)


def solution(mesh):
    return jax.shard_map(
        body,
        mesh=mesh,
        in_specs=(P(("dp", "seq"), None), P(("dp", "seq"), None), P(("dp", "seq"), None), P(), P()),
        out_specs=P(("dp", "seq"), None),
        check_vma=False,
    )
```

profile of v0, /device:TPU:1, one launch (start us, length us, event | category | flops | bytes accessed | tf_op | source)
XLA Modules:
  0.0 55.5 jit_solution(13002472010579708237)
XLA Ops:
  0.0 53.5 %dilated_attention.1 = bf16[512,768]{1,0:T(8,128)(2,1)} custom-call(s32[5,16]{1,0:T(8,128)} %off_ref.1, bf16[512,768]{1,0:T(8,128)(2,1)} %q_ref.1, bf16[512,768]{1,0:T(8,128)(2,1)} %k_ref.1, bf16[512,768]{1,0:T(8,128)(2,1)} %v_ref.1, bf16[768,768]{1,0:T(8,128)(2,1)} %w_ref.1), custom_call_target="tpu_custom_call" | custom-call | flops 3000000000 | bytes 5000000 | tf_op jit(solution)/shard_map/dilated_attention/pallas_call | solution.py:312
  53.5 2.1 %copy.7 = bf16[512,768]{1,0:T(8,128)(2,1)} copy(bf16[512,768]{1,0:T(8,128)(2,1)} %dilated_attention.1) | data formatting | bytes 1572864
where the time goes:
time: 55.7 us; the launch traced here: 55.5 us
  Pallas kernels  53.5 us (96%)
  local copies, waits for them, and re-layouts  2.06 us (4%)
    pallas_call x1, Pallas kernels, body(): pl.pallas_call(kernel, out_shape=jax.ShapeDtypeStruct((ROWS, WIDTH), BF),...  53.5 us
    unnamed x1, local copies, waits for them, and re-layouts  2.06 us

commit v1 on v0

v1 whole, which is shorter than its diff:
```python
import math

import jax
import jax.numpy as jnp
from jax import lax
from jax.experimental import pallas as pl
from jax.experimental.pallas import tpu as pltpu
from jax.sharding import PartitionSpec as P

MESH = pl.DeviceIdType.MESH
BF = jnp.bfloat16
F32 = jnp.float32
ROWS = 512
WIDTH = 768
HALF = 384
HD = 48
NH = 8
COEF = math.log2(math.e) / math.sqrt(HD)
NT = (((1,), (1,)), ((), ()))
KEPT = [ROWS >> level for level in range(5)]


def reversed_bits(x, bits):
    out = jnp.zeros_like(x)
    for b in range(bits):
        out = out + ((x >> b) & 1) * (1 << (bits - 1 - b))
    return out


def window(first, count):
    lo, hi = HD * first, HD * (first + count)
    start = lo // 128 * 128
    width = 128 if hi <= start + 128 else 256
    return start, width


def head_mask(head, start, width):
    lane = lax.broadcasted_iota(jnp.int32, (1, width), 1) + start
    return (lane >= HD * head) & (lane < HD * head + HD)


def softmax_unit(q, k, v):
    s = lax.dot_general(q, k, NT, preferred_element_type=F32)
    top = jnp.max(s, axis=1, keepdims=True) * COEF
    p = jnp.exp2(s * COEF - top)
    total = jnp.sum(p, axis=1, keepdims=True)
    o = jnp.dot(p.astype(BF), v, preferred_element_type=F32)
    return o, top, total


def kernel(
    off_ref, q_hbm, k_hbm, v_hbm, out_hbm,
    q_ref, k_ref, v_ref, stage, halves, s1, s2, s3, c4, r2, r3, q1, q2, q3, qy,
    acc0, acc1, acc2, acc3, acc4, top0, top1, top2, top3, top4,
    sum0, sum1, sum2, sum3, sum4, o3, t3, u3, o3_out, o3_in, st3_out, st3_in, st4_out, acc4_in, st4_in, m4, t4, u4,
    unperm, msend, local_sem, send_sem, recv_sem,
):
    me = lax.axis_index("seq")
    core = lax.rem(me, 2)
    z = lax.rem(me // 2, 4)
    y = me // 8

    loads = [
        pltpu.make_async_copy(src, dst, local_sem.at[i])
        for i, (src, dst) in enumerate([(k_hbm, k_ref), (v_hbm, v_ref), (q_hbm, q_ref)])
    ]
    for c in loads:
        c.start()

    def at(yy, zz, cc):
        return {"seq": (yy * 4 + zz) * 2 + cc}

    sibling = at(y, z, 1 - core)
    pair = at(y, z + 1 - 2 * lax.rem(z, 2), core)
    mirror = at(y, 3 - z, core)
    mirror_pair = at(y, 3 - (z + 1 - 2 * lax.rem(z, 2)), core)
    y_next = [at(lax.rem(y + d, 4), z, core) for d in (1, 2, 3)]
    y_back = [at(lax.rem(y + 4 - d, 4), z, core) for d in (1, 2, 3)]
    is_centre = (z + 1) // 2 == 1
    barrier = pltpu.get_barrier_semaphore()
    for peer in [sibling, pair, mirror, mirror_pair] + y_next:
        pl.semaphore_signal(barrier, inc=1, device_id=peer, device_id_type=MESH)

    def remote(send, recv, src, dst, peer):
        return pltpu.make_async_remote_copy(
            src_ref=src, dst_ref=dst, send_sem=send_sem.at[send], recv_sem=recv_sem.at[recv],
            device_id=peer, device_id_type=MESH,
        )

    kv_copy = remote(0, 0, stage.at[pl.ds(0, 2)], halves.at[1, pl.ds(0, 2)], sibling)
    q_copy = remote(1, 1, stage.at[2], halves.at[1, 2], sibling)
    l4_pair = remote(2, 2, c4.at[0], c4.at[1], pair)
    l4_mirror = remote(3, 3, c4.at[0], c4.at[2], mirror)
    l4_cross = remote(4, 4, c4.at[0], c4.at[3], mirror_pair)
    l4_fwd_mirror = remote(22, 4, c4.at[1], c4.at[3], mirror)
    l4_fwd_cross = remote(23, 3, c4.at[1], c4.at[2], mirror_pair)
    l3_pair = remote(5, 5, s3, r3.at[0], pair)
    l3_mirror = remote(6, 6, s3, r3.at[1], mirror)
    l3_fwd = remote(7, 7, r3.at[0], r3.at[2], mirror)
    n3 = 2 * KEPT[3]
    l3_q = remote(8, 8, q3.at[pl.ds(0, n3)], q3.at[pl.ds(n3, n3)], pair)
    l3_out = remote(9, 9, o3_out, o3_in, pair)
    l3_stat = remote(10, 10, st3_out, st3_in, pair)
    l2_copy = remote(11, 11, s2, r2, pair)
    n4 = 2 * KEPT[4]
    y_q = [remote(12 + i, 12 + i, qy.at[0], qy.at[i + 1], y_next[i]) for i in range(3)]
    y_acc = [remote(15 + i, 15 + i, acc4.at[pl.ds((i + 1) * n4, n4)], acc4_in.at[i], y_back[i]) for i in range(3)]
    y_stat = [remote(18 + i, 18 + i, st4_out.at[pl.ds((i + 1) * n4, n4)], st4_in.at[i], y_back[i]) for i in range(3)]

    dest = lax.broadcasted_iota(jnp.int32, (ROWS, 1), 0)
    source = (dest & 31) * 16 + reversed_bits(dest >> 5, 4)
    lane512 = lax.broadcasted_iota(jnp.int32, (ROWS, ROWS), 1)
    perm = jnp.where(lane512 == source, 1.0, 0.0).astype(BF)
    mine = pl.ds(pl.multiple_of(core * HALF, 128), HALF)
    theirs = pl.ds(pl.multiple_of((1 - core) * HALF, 128), HALF)

    def permuted(ref, lanes):
        return jnp.dot(perm, ref[:, lanes], preferred_element_type=F32).astype(BF)

    loads[0].wait()
    stage[0] = permuted(k_ref, theirs)
    loads[1].wait()
    stage[1] = permuted(v_ref, theirs)
    pl.semaphore_wait(barrier, 7)
    kv_copy.start()
    halves[0, 0] = permuted(k_ref, mine)
    halves[0, 1] = permuted(v_ref, mine)
    loads[2].wait()
    stage[2] = permuted(q_ref, theirs)
    q_copy.start()
    halves[0, 2] = permuted(q_ref, mine)

    offs = off_ref[...].astype(BF)
    head_row = lax.broadcasted_iota(jnp.int32, (16, HALF), 0)
    head_col = lax.broadcasted_iota(jnp.int32, (16, HALF), 1) // HD + NH * core
    off_cols = jnp.dot(offs, jnp.where(head_row == head_col, 1.0, 0.0).astype(BF), preferred_element_type=F32)
    stat_row = lax.broadcasted_iota(jnp.int32, (16, 128), 0)
    stat_col = (lax.broadcasted_iota(jnp.int32, (16, 128), 1) & 7) + NH * core
    off_stat = jnp.dot(offs, jnp.where(stat_row == stat_col, 1.0, 0.0).astype(BF), preferred_element_type=F32)
    block_cols, block_stat = [None], [None]
    for level in range(1, 5):
        block_cols.append(reversed_bits(off_cols[level:level + 1].astype(jnp.int32), level))
        block_stat.append(reversed_bits(off_stat[level:level + 1].astype(jnp.int32), level))

    def select(src, kind, level):
        n = KEPT[level]
        kept = halves[src, kind, 0:n]
        for b in range(1, 1 << level):
            kept = jnp.where(block_cols[level] == b, halves[src, kind, b * n:(b + 1) * n], kept)
        return kept

    for kind in range(2):
        c4[0, kind, 0:KEPT[4]] = select(0, kind, 4)
        s3[kind, 0:KEPT[3]] = select(0, kind, 3)
    q3[0:KEPT[3]] = select(0, 2, 3)
    qy[0, 0:KEPT[4]] = select(0, 2, 4)
    kv_copy.wait_recv()
    for kind in range(2):
        c4[0, kind, KEPT[4]:] = select(1, kind, 4)
    l4_pair.start()

    @pl.when(is_centre)
    def _():
        l4_mirror.start()
        l4_cross.start()

    for kind in range(2):
        s3[kind, KEPT[3]:] = select(1, kind, 3)

    @pl.when(is_centre)
    def _():
        l3_mirror.start()

    @pl.when(jnp.logical_not(is_centre))
    def _():
        l3_pair.start()

    q_copy.wait_recv()
    q3[KEPT[3]:2 * KEPT[3]] = select(1, 2, 3)
    qy[0, KEPT[4]:] = select(1, 2, 4)
    for c in y_q:
        c.start()

    @pl.when(jnp.logical_not(is_centre))
    def _():
        l3_q.start()

    for src in range(2):
        for kind in range(2):
            s2[kind, src * KEPT[2]:(src + 1) * KEPT[2]] = select(src, kind, 2)

    stat_lane = lax.broadcasted_iota(jnp.int32, (1, 128), 1) & 7

    def attend(q_of, k_of, v_of, group, rows, acc, top_ref, sum_ref, heads=(0, NH), norm=False):
        tops = jnp.zeros((rows, 128), F32) if heads[0] == 0 else top_ref[...]
        sums = jnp.zeros((rows, 128), F32) if heads[0] == 0 else sum_ref[...]
        written = {t for t in range(0, HALF, 128) if t < HD * heads[0]}
        for first in range(heads[0], heads[1], group):
            start, width = window(first, group)
            masks = [head_mask(first + g, start, width) for g in range(group)]
            q = q_of(start, width)
            if group == 1:
                stack = q
                k = jnp.where(masks[0], k_of(start, width), jnp.zeros((), BF))
            else:
                stack = jnp.concatenate([jnp.where(m, q, jnp.zeros((), BF)) for m in masks], axis=0)
                k = k_of(start, width)
            o, top, total = softmax_unit(stack, k, v_of(start, width))
            if norm:
                o = o * (1.0 / total)
            for t in range(start, start + width, 128):
                part = None
                for g in range(group):
                    lo, hi = HD * (first + g), HD * (first + g + 1)
                    if hi <= t or lo >= t + 128:
                        continue
                    piece = o[g * rows:(g + 1) * rows, t - start:t - start + 128]
                    mask = masks[g][:, t - start:t - start + 128]
                    if part is None:
                        part = jnp.where(mask, piece, acc[:, t:t + 128]) if t in written else piece
                    else:
                        part = jnp.where(mask, piece, part)
                acc[:, t:t + 128] = part
                written.add(t)
            for g in range(group):
                lanes = stat_lane == first + g
                tops = jnp.where(lanes, top[g * rows:(g + 1) * rows], tops)
                sums = jnp.where(lanes, total[g * rows:(g + 1) * rows], sums)
        top_ref[...] = tops
        sum_ref[...] = sums

    def level0(s, heads):
        attend(
            lambda a, w: halves[s, 2, :, a:a + w],
            lambda a, w: halves[s, 0, :, a:a + w],
            lambda a, w: halves[s, 1, :, a:a + w],
            1, ROWS, acc0.at[s], top0.at[s], sum0.at[s], heads,
        )

    level0(0, (0, 4))

    @pl.when(is_centre)
    def _():
        l4_pair.wait_recv()
        l4_fwd_mirror.start()
        l4_fwd_cross.start()

    level0(0, (4, 8))

    @pl.when(is_centre)
    def _():
        l3_pair.wait_recv()
        l3_fwd.start()

    l2_copy.start()
    for src in range(2):
        q2[src * KEPT[2]:(src + 1) * KEPT[2]] = select(src, 2, 2)
        q1[src * KEPT[1]:(src + 1) * KEPT[1]] = select(src, 2, 1)
        for kind in range(2):
            s1[kind, src * KEPT[1]:(src + 1) * KEPT[1]] = select(src, kind, 1)
    level0(1, (0, 8))

    @pl.when(jnp.logical_not(is_centre))
    def _():
        l4_pair.wait_recv()

    l4_mirror.wait_recv()
    l4_cross.wait_recv()
    for c in y_q:
        c.wait_recv()

    def line4(kind):
        return lambda a, w: jnp.concatenate([c4[b, kind, :, a:a + w] for b in range(4)], axis=0)

    attend(
        lambda a, w: jnp.concatenate([qy[b, :, a:a + w] for b in range(4)], axis=0),
        line4(0), line4(1), 2, 4 * n4, acc4, top4, sum4,
    )
    stat_all = lax.broadcasted_iota(jnp.int32, (1, 128), 1)
    st4_out[...] = jnp.where(stat_all < 64, top4[...], sum4[...])
    for c in y_acc + y_stat:
        c.start()
    attend(
        lambda a, w: q1[:, a:a + w], lambda a, w: s1[0, :, a:a + w], lambda a, w: s1[1, :, a:a + w],
        1, 2 * KEPT[1], acc1, top1, sum1,
    )
    back = reversed_bits(dest & 15, 4) * 32 + (dest >> 4)
    unperm[...] = jnp.where(lane512 == back, 1.0, 0.0).astype(BF)

    @pl.when(is_centre)
    def _():
        l3_mirror.wait_recv()
        l3_fwd.wait_recv()
        l3_q.wait_recv()

        def all3(kind):
            return lambda a, w: jnp.concatenate(
                [s3[kind, :, a:a + w]] + [r3[i, kind, :, a:a + w] for i in range(3)], axis=0)

        attend(lambda a, w: q3[:, a:a + w], all3(0), all3(1), 2, 2 * n3, acc3, top3, sum3, norm=True)
        o3_out[...] = acc3[n3:].astype(BF)
        st3_out[...] = jnp.where(stat_all < 16, top3[n3:], sum3[n3:]).T[0:32]
        l3_out.start()
        l3_stat.start()
        o3[...] = acc3[0:n3].astype(BF)
        t3[...] = top3[0:n3]
        u3[...] = sum3[0:n3]

    l2_copy.wait_recv()

    def both2(kind):
        return lambda a, w: jnp.concatenate([s2[kind, :, a:a + w], r2[kind, :, a:a + w]], axis=0)

    attend(lambda a, w: q2[:, a:a + w], both2(0), both2(1), 2, 2 * KEPT[2], acc2, top2, sum2)

    spread_row = lax.broadcasted_iota(jnp.int32, (128, HALF), 0)
    spread_col = lax.broadcasted_iota(jnp.int32, (128, HALF), 1) // HD
    spread = jnp.where((spread_row < 16) & ((spread_row & 7) == spread_col), 1.0, 0.0).astype(BF)

    def widened(weight):
        high = weight.astype(BF).astype(F32)
        low = jnp.where(stat_all < 16, weight - high, 0.0)
        packed = jnp.where(stat_all < 8, high, low).astype(BF)
        return jnp.dot(packed, spread, preferred_element_type=F32)

    for c in y_acc + y_stat:
        c.wait_recv()
    tops4 = [top4[0:n4]] + [st4_in[i] for i in range(3)]
    sums4 = [sum4[0:n4]] + [pltpu.roll(st4_in[i], 64, 1) for i in range(3)]
    accs4 = [acc4[0:n4]] + [acc4_in[i] for i in range(3)]
    peak4 = jnp.maximum(jnp.maximum(tops4[0], tops4[1]), jnp.maximum(tops4[2], tops4[3]))
    parts4 = [jnp.exp2(t - peak4) for t in tops4]
    t4[...] = peak4
    u4[...] = parts4[0] * sums4[0] + parts4[1] * sums4[1] + parts4[2] * sums4[2] + parts4[3] * sums4[3]
    total4 = widened(parts4[0]) * accs4[0]
    for i in range(1, 4):
        total4 = total4 + widened(parts4[i]) * accs4[i]
    m4[...] = total4

    @pl.when(jnp.logical_not(is_centre))
    def _():
        l3_out.wait_recv()
        l3_stat.wait_recv()
        o3[...] = o3_in[...]
        zeros = jnp.zeros((112, 128), F32)
        t3[...] = jnp.concatenate([st3_in[0:16], zeros], axis=0).T
        u3[...] = jnp.concatenate([st3_in[16:32], zeros], axis=0).T

    row_class = lax.broadcasted_iota(jnp.int32, (ROWS, 1), 0) >> 5
    accs = [acc0, acc1, acc2, o3, m4]
    tops = [top0, top1, top2, t3, t4]
    sums = [sum0, sum1, sum2, u3, u4]

    def merge(s):
        def full(refs, level):
            if level == 0:
                return refs[0][s]
            n = KEPT[level]
            part = refs[level][s * n:(s + 1) * n]
            return jnp.concatenate([part] * (1 << level), axis=0)

        level_tops = [full(tops, 0)]
        for level in range(1, 5):
            match = (row_class >> (4 - level)) == block_stat[level]
            level_tops.append(jnp.where(match, full(tops, level), -1e30))
        peak = level_tops[0]
        for t in level_tops[1:]:
            peak = jnp.maximum(peak, t)
        shares = [jnp.exp2(t - peak) for t in level_tops]
        weighted = [shares[level] * full(sums, level) for level in range(5)]
        inv = 1.0 / (weighted[0] + weighted[1] + weighted[2] + weighted[3] + weighted[4])
        merged = None
        for level in range(5):
            term = widened((weighted if level == 3 else shares)[level] * inv) * full(accs, level).astype(F32)
            merged = term if merged is None else merged + term
        return jnp.dot(unperm[...], merged.astype(BF), preferred_element_type=F32).astype(BF)

    msend[1] = merge(1)
    m_copy = remote(21, 21, msend.at[1], out_hbm.at[:, mine], sibling)
    m_copy.start()
    msend[0] = merge(0)
    store = pltpu.make_async_copy(msend.at[0], out_hbm.at[:, mine], local_sem.at[3])
    store.start()

    @pl.when(is_centre)
    def _():
        for c in [l4_mirror, l4_cross, l4_fwd_mirror, l4_fwd_cross, l3_mirror, l3_fwd, l3_out, l3_stat]:
            c.wait_send()

    @pl.when(jnp.logical_not(is_centre))
    def _():
        for c in [l3_pair, l3_q]:
            c.wait_send()

    for c in [kv_copy, q_copy, l4_pair, l2_copy] + y_q + y_acc + y_stat:
        c.wait_send()
    store.wait()
    m_copy.wait()


def body(queries, keys, values, offsets, out_weight):
    n = [2 * k for k in KEPT]
    bf = [
        (ROWS, WIDTH), (ROWS, WIDTH), (ROWS, WIDTH), (3, ROWS, HALF), (2, 3, ROWS, HALF),
        (2, n[1], HALF), (2, n[2], HALF), (2, n[3], HALF), (4, 2, n[4], HALF), (2, n[2], HALF), (3, 2, n[3], HALF),
        (n[1], HALF), (n[2], HALF), (2 * n[3], HALF), (4, n[4], HALF),
    ]
    scratch = [pltpu.VMEM(shape, BF) for shape in bf]
    for width in (HALF, 128, 128):
        scratch += [pltpu.VMEM(shape, F32) for shape in [
            (2, ROWS, width), (n[1], width), (n[2], width), (2 * n[3], width), (4 * n[4], width)]]
    scratch += [
        pltpu.VMEM((n[3], HALF), BF), pltpu.VMEM((n[3], 128), F32), pltpu.VMEM((n[3], 128), F32),
        pltpu.VMEM((n[3], HALF), BF), pltpu.VMEM((n[3], HALF), BF),
        pltpu.VMEM((32, 128), F32), pltpu.VMEM((32, 128), F32),
        pltpu.VMEM((4 * n[4], 128), F32), pltpu.VMEM((3, n[4], HALF), F32), pltpu.VMEM((3, n[4], 128), F32),
        pltpu.VMEM((n[4], HALF), F32), pltpu.VMEM((n[4], 128), F32), pltpu.VMEM((n[4], 128), F32),
        pltpu.VMEM((ROWS, ROWS), BF),
        pltpu.VMEM((2, ROWS, HALF), BF),
        pltpu.SemaphoreType.DMA((4,)),
        pltpu.SemaphoreType.DMA((24,)),
        pltpu.SemaphoreType.DMA((24,)),
    ]
    merged = pl.pallas_call(
        kernel,
        out_shape=jax.ShapeDtypeStruct((ROWS, WIDTH), BF),
        in_specs=[pl.BlockSpec(memory_space=pltpu.VMEM)] + [pl.BlockSpec(memory_space=pl.ANY)] * 3,
        out_specs=pl.BlockSpec(memory_space=pl.ANY),
        scratch_shapes=scratch,
        compiler_params=pltpu.CompilerParams(collective_id=0, has_side_effects=True, vmem_limit_bytes=56 << 20),
        cost_estimate=pl.CostEstimate(flops=3 * 10**9, bytes_accessed=5 * 10**6, transcendentals=9 * 10**6),
        name="dilated_attention",
    )(offsets, queries, keys, values)
    return jnp.dot(merged, out_weight, preferred_element_type=F32).astype(BF)


def solution(mesh):
    return jax.shard_map(
        body,
        mesh=mesh,
        in_specs=(P(("dp", "seq"), None), P(("dp", "seq"), None), P(("dp", "seq"), None), P(), P()),
        out_specs=P(("dp", "seq"), None),
        check_vma=False,
    )
```

time: 55.7 us -> 40.8 us (0.73)
  Pallas kernels: 53.5 us -> 37.9 us
  matrix products: 0 us -> 2.79 us
  local copies, waits for them, and re-layouts: 2.06 us -> 0.01 us
    pallas_call x1, Pallas kernels: 53.5 us -> 37.9 us  [body(): pl.pallas_call(kernel, out_shape=jax.ShapeDtypeStruct((ROWS, WIDTH), BF),...]
    dot_general x0 -> x1, matrix products: none -> 2.79 us  [body(): return jnp.dot(merged, out_weight, preferred_element_type=F32).astype(BF)]
    unnamed x1 -> x2, local copies, waits for them, and re-layouts: 2.06 us -> 0.01 us
where the time goes in v1:
time: 40.8 us; the launch traced here: 40.7 us
  Pallas kernels  37.9 us (93%)
  matrix products  2.79 us (7%)
    pallas_call x1, Pallas kernels, body(): pl.pallas_call(kernel, out_shape=jax.ShapeDtypeStruct((ROWS, WIDTH), BF),...  37.9 us
    dot_general x1, matrix products, body(): return jnp.dot(merged, out_weight, preferred_element_type=F32).astype(BF)  2.79 us

profile of v1, /device:TPU:1, one launch (start us, length us, event | category | flops | bytes accessed | tf_op | source)
XLA Modules:
  0.0 40.7 jit_solution(13369055297092816367)
XLA Ops:
  0.0 0.0 copy-start
  0.0 37.9 %dilated_attention.1 = bf16[512,768]{1,0:T(8,128)(2,1)} custom-call(s32[5,16]{1,0:T(8,128)} %off_ref.1, bf16[512,768]{1,0:T(8,128)(2,1)} %q_hbm.1, bf16[512,768]{1,0:T(8,128)(2,1)} %k_hbm.1, bf16[512,768]{1,0:T(8,128)(2,1)} %v_hbm.1), custom_call_target="tpu_custom_call" | custom-call | flops 3000000000 | bytes 5000000 | tf_op jit(solution)/shard_map/dilated_attention/pallas_call | solution.py:424
  37.9 0.0 copy-done
  37.9 2.8 %convolution_convert_fusion = bf16[512,768]{1,0:T(8,128)(2,1)} fusion(bf16[512,768]{1,0:T(8,128)(2,1)} %dilated_attention.1, bf16[768,768]{1,0:T(8,128)(2,1)S(1)} %copy-done), kind=kOutput, calls=%fused_computation | convolution fusion | flops 604372992 | bytes 2752512 | tf_op jit(solution)/shard_map/dot_general | solution.py:434
Async XLA Ops:
  0.0 37.9 %copy-start = (bf16[768,768]{1,0:T(8,128)(2,1)S(1)}, bf16[768,768]{1,0:T(8,128)(2,1)}, u32[]{:S(2)}) copy-start(bf16[768,768]{1,0:T(8,128)(2,1)} %param.9) | copy-start | bytes 3538948

commit v2 on v1

v2 whole, which is shorter than its diff:
```python
import math

import jax
import jax.numpy as jnp
from jax import lax
from jax.experimental import pallas as pl
from jax.experimental.pallas import tpu as pltpu
from jax.sharding import PartitionSpec as P

MESH = pl.DeviceIdType.MESH
BF = jnp.bfloat16
F32 = jnp.float32
ROWS = 512
WIDTH = 768
HALF = 384
HD = 48
NH = 8
COEF = math.log2(math.e) / math.sqrt(HD)
NT = (((1,), (1,)), ((), ()))
KEPT = [ROWS >> level for level in range(5)]


def reversed_bits(x, bits):
    out = jnp.zeros_like(x)
    for b in range(bits):
        out = out + ((x >> b) & 1) * (1 << (bits - 1 - b))
    return out


def window(first, count):
    lo, hi = HD * first, HD * (first + count)
    start = lo // 128 * 128
    width = 128 if hi <= start + 128 else 256
    return start, width


def head_mask(head, start, width):
    lane = lax.broadcasted_iota(jnp.int32, (1, width), 1) + start
    return (lane >= HD * head) & (lane < HD * head + HD)


def softmax_unit(q, k, v):
    s = lax.dot_general(q, k, NT, preferred_element_type=F32)
    top = jnp.max(s, axis=1, keepdims=True) * COEF
    p = jnp.exp2(s * COEF - top)
    total = jnp.sum(p, axis=1, keepdims=True)
    o = jnp.dot(p.astype(BF), v, preferred_element_type=F32)
    return o, top, total


def kernel(
    off_hbm, q_hbm, k_hbm, v_hbm, out_ref,
    off_ref, q_ref, k_ref, v_ref, stage, halves, s1, c2, c3, c4, x2, x3, x4, q1, q2, q3, qy,
    acc0, acc1, acc2, acc3, acc4, top0, top1, top2, top3, top4,
    sum0, sum1, sum2, sum3, sum4, o3, t3, u3, o3_out, o3_in, st3_out, st3_in, acc4_out, st4_out, acc4_in, st4_in, m4, t4, u4,
    unperm, msend, local_sem, send_sem, recv_sem,
):
    me = lax.axis_index("seq")
    core = lax.rem(me, 2)
    z = lax.rem(me // 2, 4)
    y = me // 8

    loads = [
        pltpu.make_async_copy(src, dst, local_sem.at[i])
        for i, (src, dst) in enumerate([(k_hbm, k_ref), (v_hbm, v_ref), (q_hbm, q_ref), (off_hbm, off_ref)])
    ]
    for i in (3, 0, 1, 2):
        loads[i].start()

    def at(yy, zz, cc):
        return {"seq": (yy * 4 + zz) * 2 + cc}

    z_pair = z + 1 - 2 * lax.rem(z, 2)
    sibling = at(y, z, 1 - core)
    pair, pair_other = at(y, z_pair, core), at(y, z_pair, 1 - core)
    mirror, mirror_other = at(y, 3 - z, core), at(y, 3 - z, 1 - core)
    y_next = [at(lax.rem(y + d, 4), z, core) for d in (1, 2, 3)]
    y_back = [at(lax.rem(y + 4 - d, 4), z, core) for d in (1, 2, 3)]
    is_centre = (z + 1) // 2 == 1
    is_end = jnp.logical_not(is_centre)
    barrier = pltpu.get_barrier_semaphore()
    for peer in [sibling, pair, pair_other, mirror, mirror_other] + y_next:
        pl.semaphore_signal(barrier, inc=1, device_id=peer, device_id_type=MESH)

    def remote(send, recv, src, dst, peer):
        return pltpu.make_async_remote_copy(
            src_ref=src, dst_ref=dst, send_sem=send_sem.at[send], recv_sem=recv_sem.at[recv],
            device_id=peer, device_id_type=MESH,
        )

    kv_copy = remote(0, 0, stage.at[pl.ds(0, 2)], halves.at[1, pl.ds(0, 2)], sibling)
    q_copy = remote(1, 1, stage.at[2], halves.at[1, 2], sibling)
    def spread_out(first, slots, extra):
        return [
            remote(first, first, extra, slots.at[0, core], sibling),
            remote(first + 1, first + 1, slots.at[0, core], slots.at[1, core], pair),
            remote(first + 2, first + 2, extra, slots.at[1, core], pair_other),
        ]

    def to_mirror(first, slots, extra):
        return [
            remote(first, first, slots.at[0, core], slots.at[2, core], mirror),
            remote(first + 1, first + 1, extra, slots.at[2, core], mirror_other),
        ]

    l4_sib, *l4_pair = spread_out(2, c4, x4)
    l3_sib, *l3_pair = spread_out(5, c3, x3)
    l2_sib = remote(8, 8, x2, c2.at[0, core], sibling)
    l2_pair = []
    for t in range(3):
        tile = pl.ds(128 * t, 128)
        l2_pair += [
            remote(9 + 2 * t, 9 + 2 * t, c2.at[0, core, :, :, tile], c2.at[1, core, :, :, tile], pair),
            remote(10 + 2 * t, 10 + 2 * t, x2.at[:, :, tile], c2.at[1, core, :, :, tile], pair_other),
        ]
    l4_mirror = to_mirror(15, c4, x4)
    l3_mirror = to_mirror(17, c3, x3)
    l4_fwd_mirror = remote(19, 19, c4.at[1], c4.at[3], mirror)
    l4_fwd_pair2 = remote(20, 19, c4.at[2], c4.at[3], pair)
    l4_fwd_pair3 = remote(21, 20, c4.at[3], c4.at[2], pair)
    l3_fwd = remote(22, 21, c3.at[1], c3.at[3], mirror)
    n3 = 2 * KEPT[3]
    l3_q = remote(23, 22, q3.at[pl.ds(0, n3)], q3.at[pl.ds(n3, n3)], pair)
    l3_out = remote(24, 23, o3_out, o3_in, pair)
    l3_stat = remote(25, 24, st3_out, st3_in, pair)
    n4 = 2 * KEPT[4]
    y_q = [remote(26 + i, 26 + i, qy.at[0], qy.at[i + 1], y_next[i]) for i in range(3)]
    y_acc = [remote(29 + i, 29 + i, acc4_out.at[pl.ds(i * n4, n4)], acc4_in.at[i], y_back[i]) for i in range(3)]
    y_stat = [remote(32 + i, 32 + i, st4_out.at[(i + 1) // 2], st4_in.at[i], y_back[i]) for i in range(3)]
    m_copy = remote(35, 35, msend, out_ref.at[:, pl.ds(pl.multiple_of(core * HALF, 128), HALF)], sibling)

    dest = lax.broadcasted_iota(jnp.int32, (ROWS, 1), 0)
    source = (dest & 31) * 16 + reversed_bits(dest >> 5, 4)
    lane512 = lax.broadcasted_iota(jnp.int32, (ROWS, ROWS), 1)
    perm = jnp.where(lane512 == source, 1.0, 0.0).astype(BF)
    mine = pl.ds(pl.multiple_of(core * HALF, 128), HALF)
    theirs = pl.ds(pl.multiple_of((1 - core) * HALF, 128), HALF)

    def permuted(ref, lanes):
        return jnp.dot(perm, ref[:, lanes], preferred_element_type=F32).astype(BF)

    loads[3].wait()
    offs = off_ref[...].astype(BF)

    def reversed_offsets(heads):
        row = lax.broadcasted_iota(jnp.int32, heads.shape, 0)
        spread = jnp.dot(offs, jnp.where(row == heads, 1.0, 0.0).astype(BF), preferred_element_type=F32)
        return [None] + [reversed_bits(spread[level:level + 1].astype(jnp.int32), level) for level in range(1, 5)]

    column = lax.broadcasted_iota(jnp.int32, (16, HALF), 1) // HD
    mine_cols = reversed_offsets(column + NH * core)
    theirs_cols = reversed_offsets(column + NH * (1 - core))
    block_stat = reversed_offsets((lax.broadcasted_iota(jnp.int32, (16, 128), 1) & 7) + NH * core)

    def select(block, cols, level):
        n = KEPT[level]
        kept = block[0:n]
        for b in range(1, 1 << level):
            kept = jnp.where(cols[level] == b, block[b * n:(b + 1) * n], kept)
        return kept

    for kind, ref in enumerate([k_ref, v_ref]):
        loads[kind].wait()
        halves[0, kind] = permuted(ref, mine)
        stage[kind] = permuted(ref, theirs)
        c4[0, core, kind] = select(halves.at[0, kind], mine_cols, 4)
        x4[kind] = select(stage.at[kind], theirs_cols, 4)
    pl.semaphore_wait(barrier, 8)
    for c in l4_pair:
        c.start()

    @pl.when(is_centre)
    def _():
        for c in l4_mirror:
            c.start()

    for kind in range(2):
        c3[0, core, kind] = select(halves.at[0, kind], mine_cols, 3)
        x3[kind] = select(stage.at[kind], theirs_cols, 3)

    @pl.when(is_centre)
    def _():
        for c in l3_mirror:
            c.start()

    @pl.when(is_end)
    def _():
        for c in l3_pair:
            c.start()

    l4_sib.start()
    l3_sib.start()
    kv_copy.start()
    loads[2].wait()
    stage[2] = permuted(q_ref, theirs)
    q_copy.start()
    for kind in range(2):
        c2[0, core, kind] = select(halves.at[0, kind], mine_cols, 2)
        x2[kind] = select(stage.at[kind], theirs_cols, 2)

    @pl.when(is_centre)
    def _():
        for c in l2_pair:
            c.start()

    l2_sib.start()
    halves[0, 2] = permuted(q_ref, mine)
    for src in range(2):
        if src == 1:
            q_copy.wait_recv()
        block = halves.at[src, 2]
        qy[0, src * KEPT[4]:(src + 1) * KEPT[4]] = select(block, mine_cols, 4)
        q3[src * KEPT[3]:(src + 1) * KEPT[3]] = select(block, mine_cols, 3)
    for c in y_q:
        c.start()

    @pl.when(is_end)
    def _():
        l3_q.start()

    stat_lane = lax.broadcasted_iota(jnp.int32, (1, 128), 1) & 7

    def attend(q_of, k_of, v_of, group, rows, acc, top_ref, sum_ref, heads=(0, NH), norm=False):
        tops = jnp.zeros((rows, 128), F32) if heads[0] == 0 else top_ref[...]
        sums = jnp.zeros((rows, 128), F32) if heads[0] == 0 else sum_ref[...]
        written = {t for t in range(0, HALF, 128) if t < HD * heads[0]}
        for first in range(heads[0], heads[1], group):
            start, width = window(first, group)
            masks = [head_mask(first + g, start, width) for g in range(group)]
            q = q_of(start, width)
            if group == 1:
                stack = q
                k = jnp.where(masks[0], k_of(start, width), jnp.zeros((), BF))
            else:
                stack = jnp.concatenate([jnp.where(m, q, jnp.zeros((), BF)) for m in masks], axis=0)
                k = k_of(start, width)
            o, top, total = softmax_unit(stack, k, v_of(start, width))
            if norm:
                o = o * (1.0 / total)
            for t in range(start, start + width, 128):
                part = None
                for g in range(group):
                    lo, hi = HD * (first + g), HD * (first + g + 1)
                    if hi <= t or lo >= t + 128:
                        continue
                    piece = o[g * rows:(g + 1) * rows, t - start:t - start + 128]
                    mask = masks[g][:, t - start:t - start + 128]
                    if part is None:
                        part = jnp.where(mask, piece, acc[:, t:t + 128]) if t in written else piece
                    else:
                        part = jnp.where(mask, piece, part)
                acc[:, t:t + 128] = part
                written.add(t)
            for g in range(group):
                lanes = stat_lane == first + g
                tops = jnp.where(lanes, top[g * rows:(g + 1) * rows], tops)
                sums = jnp.where(lanes, total[g * rows:(g + 1) * rows], sums)
        top_ref[...] = tops
        sum_ref[...] = sums

    def level0(s, heads):
        attend(
            lambda a, w: halves[s, 2, :, a:a + w],
            lambda a, w: halves[s, 0, :, a:a + w],
            lambda a, w: halves[s, 1, :, a:a + w],
            1, ROWS, acc0.at[s], top0.at[s], sum0.at[s], heads,
        )

    level0(0, (0, 4))

    @pl.when(is_centre)
    def _():
        for c in l4_pair:
            c.wait_recv()
        l4_fwd_mirror.start()
        for c in l4_mirror:
            c.wait_recv()
        l4_fwd_pair2.start()

    level0(0, (4, NH))
    kv_copy.wait_recv()
    level0(1, (0, 4))

    @pl.when(is_centre)
    def _():
        for c in l3_pair:
            c.wait_recv()
        l3_fwd.start()
        l4_fwd_mirror.wait_recv()
        l4_fwd_pair3.start()

    @pl.when(is_end)
    def _():
        for c in l3_pair:
            c.wait_send()
        for c in l2_pair:
            c.start()

    level0(1, (4, NH))
    for src in range(2):
        q2[src * KEPT[2]:(src + 1) * KEPT[2]] = select(halves.at[src, 2], mine_cols, 2)
        q1[src * KEPT[1]:(src + 1) * KEPT[1]] = select(halves.at[src, 2], mine_cols, 1)
        for kind in range(2):
            s1[kind, src * KEPT[1]:(src + 1) * KEPT[1]] = select(halves.at[src, kind], mine_cols, 1)

    def level1(heads):
        attend(
            lambda a, w: q1[:, a:a + w], lambda a, w: s1[0, :, a:a + w], lambda a, w: s1[1, :, a:a + w],
            1, 2 * KEPT[1], acc1, top1, sum1, heads,
        )

    level1((0, 4))

    @pl.when(is_end)
    def _():
        for c in l4_pair:
            c.wait_recv()
        l4_fwd_pair2.wait_recv()
        l4_fwd_pair3.wait_recv()

    l4_sib.wait_recv()
    for c in y_q:
        c.wait_recv()

    def chips(ref, kind, slots):
        return lambda a, w: jnp.concatenate(
            [ref[slot, tok, kind, :, a:a + w] for slot in range(slots) for tok in range(2)], axis=0)

    attend(
        lambda a, w: jnp.concatenate([qy[b, :, a:a + w] for b in range(4)], axis=0),
        chips(c4, 0, 4), chips(c4, 1, 4), 2, 4 * n4, acc4, top4, sum4, norm=True,
    )
    stat_all = lax.broadcasted_iota(jnp.int32, (1, 128), 1)
    acc4_out[...] = acc4[n4:].astype(BF)
    packed4 = jnp.where(stat_all < 16, top4[...], sum4[...])
    for i in range(2):
        st4_out[i] = packed4[128 * i:128 * (i + 1)].T[0:32]
    for c in y_acc + y_stat:
        c.start()
    level1((4, NH))
    back = reversed_bits(dest & 15, 4) * 32 + (dest >> 4)
    unperm[...] = jnp.where(lane512 == back, 1.0, 0.0).astype(BF)

    l3_sib.wait_recv()

    @pl.when(is_centre)
    def _():
        for c in l3_mirror:
            c.wait_recv()
        l3_fwd.wait_recv()
        l3_q.wait_recv()
        attend(lambda a, w: q3[:, a:a + w], chips(c3, 0, 4), chips(c3, 1, 4), 2, 2 * n3, acc3, top3, sum3, norm=True)
        o3_out[...] = acc3[n3:].astype(BF)
        st3_out[...] = jnp.where(stat_all < 16, top3[n3:], sum3[n3:]).T[0:32]
        l3_out.start()
        l3_stat.start()
        o3[...] = acc3[0:n3].astype(BF)
        t3[...] = top3[0:n3]
        u3[...] = sum3[0:n3]

    row_class = lax.broadcasted_iota(jnp.int32, (ROWS, 1), 0) >> 5

    def full(ref, level, s):
        n = KEPT[level]
        return jnp.concatenate([ref[s * n:(s + 1) * n]] * (1 << level), axis=0)

    def full_top(ref, level, s):
        match = (row_class >> (4 - level)) == block_stat[level]
        return jnp.where(match, full(ref, level, s), -1e30)

    spread_row = lax.broadcasted_iota(jnp.int32, (128, HALF), 0)
    spread_col = lax.broadcasted_iota(jnp.int32, (128, HALF), 1) // HD
    spread = jnp.where((spread_row < 16) & ((spread_row & 7) == spread_col), 1.0, 0.0).astype(BF)

    def widened(weight):
        high = weight.astype(BF).astype(F32)
        low = jnp.where(stat_all < 16, weight - high, 0.0)
        packed = jnp.where(stat_all < 8, high, low).astype(BF)
        return jnp.dot(packed, spread, preferred_element_type=F32)

    for src in range(2):
        other = full_top(top1, 1, src)
        peak = jnp.maximum(top0[src], other)
        share0, share1 = jnp.exp2(top0[src] - peak), jnp.exp2(other - peak)
        top0[src] = peak
        sum0[src] = share0 * sum0[src] + share1 * full(sum1, 1, src)
        acc0[src] = widened(share0) * acc0[src] + widened(share1) * full(acc1, 1, src)

    l2_sib.wait_recv()
    for tile in range(3):
        for c in l2_pair[2 * tile:2 * tile + 2]:
            c.wait_recv()
        attend(
            lambda a, w: q2[:, a:a + w], chips(c2, 0, 2), chips(c2, 1, 2), 2, 2 * KEPT[2], acc2, top2, sum2,
            ((0, 2), (2, 4), (4, NH))[tile],
        )

    for c in y_acc + y_stat:
        c.wait_recv()
    zeros = jnp.zeros((112, 128), F32)

    def unpacked(stat):
        return [jnp.concatenate([stat[16 * i:16 * (i + 1)], zeros], axis=0).T for i in range(2)]

    tops4, sums4, accs4 = [top4[0:n4]], [sum4[0:n4]], [acc4[0:n4]]
    for i in range(3):
        at4 = (i + 1) % 2 * n4
        for part, stats in zip(unpacked(st4_in.at[i]), (tops4, sums4)):
            stats.append(part[at4:at4 + n4])
        accs4.append(acc4_in[i].astype(F32))
    peak4 = jnp.maximum(jnp.maximum(tops4[0], tops4[1]), jnp.maximum(tops4[2], tops4[3]))
    parts4 = [jnp.exp2(t - peak4) * total for t, total in zip(tops4, sums4)]
    t4[...] = peak4
    u4[...] = parts4[0] + parts4[1] + parts4[2] + parts4[3]
    total4 = widened(parts4[0]) * accs4[0]
    for i in range(1, 4):
        total4 = total4 + widened(parts4[i]) * accs4[i]
    m4[...] = total4

    @pl.when(is_end)
    def _():
        l3_out.wait_recv()
        l3_stat.wait_recv()
        o3[...] = o3_in[...]
        t3[...], u3[...] = unpacked(st3_in)

    rest = [(2, acc2, top2, sum2), (3, o3, t3, u3), (4, m4, t4, u4)]

    def merge(s):
        level_tops = [top0[s]] + [full_top(top, level, s) for level, _, top, _ in rest]
        peak = jnp.maximum(jnp.maximum(level_tops[0], level_tops[1]), jnp.maximum(level_tops[2], level_tops[3]))
        shares = [jnp.exp2(t - peak) for t in level_tops]
        weighted = [shares[0] * sum0[s]]
        for share, (level, _, _, total) in zip(shares[1:], rest):
            weighted.append(share * full(total, level, s))
        inv = 1.0 / (weighted[0] + weighted[1] + weighted[2] + weighted[3])
        merged = widened(shares[0] * inv) * acc0[s]
        for i, (level, acc, _, _) in enumerate(rest):
            factor = widened((weighted if level == 3 else shares)[i + 1] * inv)
            merged = merged + factor * full(acc, level, s).astype(F32)
        return jnp.dot(unperm[...], merged.astype(BF), preferred_element_type=F32).astype(BF)

    msend[...] = merge(1)
    m_copy.start()
    out_ref[:, mine] = merge(0)

    @pl.when(is_centre)
    def _():
        for c in l4_mirror + l3_mirror + [l4_fwd_mirror, l4_fwd_pair2, l4_fwd_pair3, l3_fwd, l3_out, l3_stat]:
            c.wait_send()

    @pl.when(is_end)
    def _():
        l3_q.wait_send()

    for c in [kv_copy, q_copy, l4_sib, l3_sib, l2_sib] + l4_pair + l2_pair + y_q + y_acc + y_stat:
        c.wait_send()
    m_copy.wait()


def project(merged_ref, w_ref, out_hbm, out_ref, sem):
    half = ROWS // 2
    stores = []
    for i in range(2):
        rows = pl.ds(i * half, half)
        out_ref[rows] = jnp.dot(merged_ref[rows], w_ref[...], preferred_element_type=F32).astype(BF)
        stores.append(pltpu.make_async_copy(out_ref.at[rows], out_hbm.at[rows], sem.at[i]))
        stores[i].start()
    for c in stores:
        c.wait()


def body(queries, keys, values, offsets, out_weight):
    n = [2 * k for k in KEPT]
    bf = [
        (ROWS, WIDTH), (ROWS, WIDTH), (ROWS, WIDTH), (3, ROWS, HALF), (2, 3, ROWS, HALF), (2, n[1], HALF),
        (2, 2, 2, KEPT[2], HALF), (4, 2, 2, KEPT[3], HALF), (4, 2, 2, KEPT[4], HALF),
        (2, KEPT[2], HALF), (2, KEPT[3], HALF), (2, KEPT[4], HALF),
        (n[1], HALF), (n[2], HALF), (2 * n[3], HALF), (4, n[4], HALF),
    ]
    scratch = [pltpu.VMEM((5, 16), jnp.int32)] + [pltpu.VMEM(shape, BF) for shape in bf]
    for width in (HALF, 128, 128):
        scratch += [pltpu.VMEM(shape, F32) for shape in [
            (2, ROWS, width), (n[1], width), (n[2], width), (2 * n[3], width), (4 * n[4], width)]]
    scratch += [
        pltpu.VMEM((n[3], HALF), BF), pltpu.VMEM((n[3], 128), F32), pltpu.VMEM((n[3], 128), F32),
        pltpu.VMEM((n[3], HALF), BF), pltpu.VMEM((n[3], HALF), BF),
        pltpu.VMEM((32, 128), F32), pltpu.VMEM((32, 128), F32),
        pltpu.VMEM((3 * n[4], HALF), BF), pltpu.VMEM((2, 32, 128), F32), pltpu.VMEM((3, n[4], HALF), BF), pltpu.VMEM((3, 32, 128), F32),
        pltpu.VMEM((n[4], HALF), F32), pltpu.VMEM((n[4], 128), F32), pltpu.VMEM((n[4], 128), F32),
        pltpu.VMEM((ROWS, ROWS), BF),
        pltpu.VMEM((ROWS, HALF), BF),
        pltpu.SemaphoreType.DMA((4,)),
        pltpu.SemaphoreType.DMA((36,)),
        pltpu.SemaphoreType.DMA((36,)),
    ]
    vmem = pl.BlockSpec(memory_space=pltpu.VMEM)
    anywhere = pl.BlockSpec(memory_space=pl.ANY)
    merged = pl.pallas_call(
        kernel,
        out_shape=pltpu.VMEM((ROWS, WIDTH), BF),
        in_specs=[anywhere] * 4,
        out_specs=vmem,
        scratch_shapes=scratch,
        compiler_params=pltpu.CompilerParams(collective_id=0, has_side_effects=True, vmem_limit_bytes=40 << 20),
        cost_estimate=pl.CostEstimate(flops=3 * 10**9, bytes_accessed=5 * 10**6, transcendentals=9 * 10**6),
        name="dilated_attention",
    )(*[pltpu.with_memory_space_constraint(x, pltpu.HBM) for x in (offsets, queries, keys, values)])
    return pl.pallas_call(
        project,
        out_shape=jax.ShapeDtypeStruct((ROWS, WIDTH), BF),
        in_specs=[vmem, vmem],
        out_specs=anywhere,
        scratch_shapes=[pltpu.VMEM((ROWS, WIDTH), BF), pltpu.SemaphoreType.DMA((2,))],
        compiler_params=pltpu.CompilerParams(vmem_limit_bytes=16 << 20),
        name="projection",
    )(merged, pltpu.with_memory_space_constraint(out_weight, pltpu.VMEM))


def solution(mesh):
    return jax.shard_map(
        body,
        mesh=mesh,
        in_specs=(P(("dp", "seq"), None), P(("dp", "seq"), None), P(("dp", "seq"), None), P(), P()),
        out_specs=P(("dp", "seq"), None),
        check_vma=False,
    )
```

time: 40.8 us -> 34.6 us (0.85)
  Pallas kernels: 37.9 us -> 34.4 us
  matrix products: 2.79 us -> 0 us
    pallas_call x1 -> x2, Pallas kernels: 37.9 us -> 34.4 us  [the longest x1 32.8 us: body(): pl.pallas_call(kernel, out_shape=pltpu.VMEM((ROWS, WIDTH), BF), in_specs=...]
    dot_general x1 -> x0, matrix products: 2.79 us -> none  [body(): return jnp.dot(merged, out_weight, preferred_element_type=F32).astype(BF)]
where the time goes in v2:
time: 34.6 us
  Pallas kernels  34.4 us (99%)
    pallas_call x1, Pallas kernels, body(): pl.pallas_call(kernel, out_shape=pltpu.VMEM((ROWS, WIDTH), BF), in_specs=...  32.8 us
    pallas_call x1, Pallas kernels, body(): pl.pallas_call(project, out_shape=jax.ShapeDtypeStruct((ROWS, WIDTH), BF)...  1.54 us

profile of v2, /device:TPU:1, one launch (start us, length us, event | category | flops | bytes accessed | tf_op | source)
XLA Modules:
  0.0 34.6 jit_solution(9241294466495015229)
XLA Ops:
  0.0 0.0 copy-start
  0.0 32.8 %dilated_attention.1.merged_ref = bf16[512,768]{1,0:T(8,128)(2,1)S(1)} custom-call(s32[5,16]{1,0:T(8,128)} %off_hbm.1, bf16[512,768]{1,0:T(8,128)(2,1)} %q_hbm.1, bf16[512,768]{1,0:T(8,128)(2,1)} %k_hbm.1, bf16[512,768]{1,0:T(8,128)(2,1)} %v_hbm.1), custom_call_target="tpu_custom_call" | custom-call | flops 3000000000 | bytes 5000000 | tf_op jit(solution)/shard_map/dilated_attention/pallas_call | solution.py:499
  32.8 0.0 copy-done
  32.9 1.5 %projection.1 = bf16[512,768]{1,0:T(8,128)(2,1)} custom-call(bf16[512,768]{1,0:T(8,128)(2,1)S(1)} %dilated_attention.1.merged_ref, bf16[768,768]{1,0:T(8,128)(2,1)S(1)} %copy-done), custom_call_target="tpu_custom_call" | custom-call | tf_op jit(solution)/shard_map/projection/pallas_call | solution.py:509
Async XLA Ops:
  0.0 32.9 %copy-start = (bf16[768,768]{1,0:T(8,128)(2,1)S(1)}, bf16[768,768]{1,0:T(8,128)(2,1)}, u32[]{:S(2)}) copy-start(bf16[768,768]{1,0:T(8,128)(2,1)} %w_ref.1) | copy-start | bytes 3538948

commit v3 on v2

--- a/solution.py
+++ b/solution.py
@@ -39,8 +39,7 @@
     return (lane >= HD * head) & (lane < HD * head + HD)
 
 
-def softmax_unit(q, k, v):
-    s = lax.dot_general(q, k, NT, preferred_element_type=F32)
+def softmax_unit(s, v):
     top = jnp.max(s, axis=1, keepdims=True) * COEF
     p = jnp.exp2(s * COEF - top)
     total = jnp.sum(p, axis=1, keepdims=True)
@@ -117,7 +116,6 @@
     l3_mirror = to_mirror(17, c3, x3)
     l4_fwd_mirror = remote(19, 19, c4.at[1], c4.at[3], mirror)
     l4_fwd_pair2 = remote(20, 19, c4.at[2], c4.at[3], pair)
-    l4_fwd_pair3 = remote(21, 20, c4.at[3], c4.at[2], pair)
     l3_fwd = remote(22, 21, c3.at[1], c3.at[3], mirror)
     n3 = 2 * KEPT[3]
     l3_q = remote(23, 22, q3.at[pl.ds(0, n3)], q3.at[pl.ds(n3, n3)], pair)
@@ -166,13 +164,8 @@
         c4[0, core, kind] = select(halves.at[0, kind], mine_cols, 4)
         x4[kind] = select(stage.at[kind], theirs_cols, 4)
     pl.semaphore_wait(barrier, 8)
-    for c in l4_pair:
+    for c in l4_pair + l4_mirror:
         c.start()
-
-    @pl.when(is_centre)
-    def _():
-        for c in l4_mirror:
-            c.start()
 
     for kind in range(2):
         c3[0, core, kind] = select(halves.at[0, kind], mine_cols, 3)
@@ -224,17 +217,25 @@
         tops = jnp.zeros((rows, 128), F32) if heads[0] == 0 else top_ref[...]
         sums = jnp.zeros((rows, 128), F32) if heads[0] == 0 else sum_ref[...]
         written = {t for t in range(0, HALF, 128) if t < HD * heads[0]}
+
+        def scores(first):
+            start, width = window(first, group)
+            masks = [head_mask(first + g, start, width) for g in range(group)]
+            q, k = q_of(start, width), k_of(start, width)
+            if group == 1:
+                k = jnp.where(masks[0], k, jnp.zeros((), BF))
+            else:
+                q = jnp.concatenate([jnp.where(m, q, jnp.zeros((), BF)) for m in masks], axis=0)
+            return lax.dot_general(q, k, NT, preferred_element_type=F32)
+
+        following = scores(heads[0])
         for first in range(heads[0], heads[1], group):
             start, width = window(first, group)
             masks = [head_mask(first + g, start, width) for g in range(group)]
-            q = q_of(start, width)
-            if group == 1:
-                stack = q
-                k = jnp.where(masks[0], k_of(start, width), jnp.zeros((), BF))
-            else:
-                stack = jnp.concatenate([jnp.where(m, q, jnp.zeros((), BF)) for m in masks], axis=0)
-                k = k_of(start, width)
-            o, top, total = softmax_unit(stack, k, v_of(start, width))
+            s = following
+            if first + group < heads[1]:
+                following = scores(first + group)
+            o, top, total = softmax_unit(s, v_of(start, width))
             if norm:
                 o = o * (1.0 / total)
             for t in range(start, start + width, 128):
@@ -278,6 +279,7 @@
         l4_fwd_pair2.start()
 
     level0(0, (4, NH))
+
     kv_copy.wait_recv()
     level0(1, (0, 4))
 
@@ -286,8 +288,6 @@
         for c in l3_pair:
             c.wait_recv()
         l3_fwd.start()
-        l4_fwd_mirror.wait_recv()
-        l4_fwd_pair3.start()
 
     @pl.when(is_end)
     def _():
@@ -311,12 +311,17 @@
 
     level1((0, 4))
 
+    @pl.when(is_centre)
+    def _():
+        l4_fwd_mirror.wait_recv()
+
     @pl.when(is_end)
     def _():
         for c in l4_pair:
             c.wait_recv()
+        for c in l4_mirror:
+            c.wait_recv()
         l4_fwd_pair2.wait_recv()
-        l4_fwd_pair3.wait_recv()
 
     l4_sib.wait_recv()
     for c in y_q:
@@ -337,11 +342,14 @@
         st4_out[i] = packed4[128 * i:128 * (i + 1)].T[0:32]
     for c in y_acc + y_stat:
         c.start()
-    level1((4, NH))
-    back = reversed_bits(dest & 15, 4) * 32 + (dest >> 4)
-    unperm[...] = jnp.where(lane512 == back, 1.0, 0.0).astype(BF)
-
     l3_sib.wait_recv()
+
+    def level3(start):
+        rows = pl.ds(start, n3)
+        attend(
+            lambda a, w: q3[rows, a:a + w], chips(c3, 0, 4), chips(c3, 1, 4),
+            4, n3, acc3.at[rows], top3.at[rows], sum3.at[rows], norm=True,
+        )
 
     @pl.when(is_centre)
     def _():
@@ -349,11 +357,19 @@
             c.wait_recv()
         l3_fwd.wait_recv()
         l3_q.wait_recv()
-        attend(lambda a, w: q3[:, a:a + w], chips(c3, 0, 4), chips(c3, 1, 4), 2, 2 * n3, acc3, top3, sum3, norm=True)
+        level3(n3)
         o3_out[...] = acc3[n3:].astype(BF)
         st3_out[...] = jnp.where(stat_all < 16, top3[n3:], sum3[n3:]).T[0:32]
         l3_out.start()
         l3_stat.start()
+
+    level1((4, NH))
+    back = reversed_bits(dest & 15, 4) * 32 + (dest >> 4)
+    unperm[...] = jnp.where(lane512 == back, 1.0, 0.0).astype(BF)
+
+    @pl.when(is_centre)
+    def _():
+        level3(0)
         o3[...] = acc3[0:n3].astype(BF)
         t3[...] = top3[0:n3]
         u3[...] = sum3[0:n3]
@@ -446,14 +462,14 @@
 
     @pl.when(is_centre)
     def _():
-        for c in l4_mirror + l3_mirror + [l4_fwd_mirror, l4_fwd_pair2, l4_fwd_pair3, l3_fwd, l3_out, l3_stat]:
+        for c in l3_mirror + [l4_fwd_mirror, l4_fwd_pair2, l3_fwd, l3_out, l3_stat]:
             c.wait_send()
 
     @pl.when(is_end)
     def _():
         l3_q.wait_send()
 
-    for c in [kv_copy, q_copy, l4_sib, l3_sib, l2_sib] + l4_pair + l2_pair + y_q + y_acc + y_stat:
+    for c in [kv_copy, q_copy, l4_sib, l3_sib, l2_sib] + l4_pair + l4_mirror + l2_pair + y_q + y_acc + y_stat:
         c.wait_send()
     m_copy.wait()
 

time: 34.6 us -> 34.1 us (0.986)
  Pallas kernels: 34.4 us -> 33.8 us
    pallas_call x1, Pallas kernels: 32.8 us -> 32.3 us  [body(): pl.pallas_call(kernel, out_shape=pltpu.VMEM((ROWS, WIDTH), BF), in_specs=...]
where the time goes in v3:
time: 34.1 us; the launch traced here: 34 us
  Pallas kernels  33.8 us (99%)
    pallas_call x1, Pallas kernels, body(): pl.pallas_call(kernel, out_shape=pltpu.VMEM((ROWS, WIDTH), BF), in_specs=...  32.3 us
    pallas_call x1, Pallas kernels, body(): pl.pallas_call(project, out_shape=jax.ShapeDtypeStruct((ROWS, WIDTH), BF)...  1.54 us

profile of v3, /device:TPU:1, one launch (start us, length us, event | category | flops | bytes accessed | tf_op | source)
XLA Modules:
  0.0 34.0 jit_solution(3912029961731877275)
XLA Ops:
  0.0 0.0 copy-start
  0.0 32.3 %dilated_attention.1.merged_ref = bf16[512,768]{1,0:T(8,128)(2,1)S(1)} custom-call(s32[5,16]{1,0:T(8,128)} %off_hbm.1, bf16[512,768]{1,0:T(8,128)(2,1)} %q_hbm.1, bf16[512,768]{1,0:T(8,128)(2,1)} %k_hbm.1, bf16[512,768]{1,0:T(8,128)(2,1)} %v_hbm.1), custom_call_target="tpu_custom_call" | custom-call | flops 3000000000 | bytes 5000000 | tf_op jit(solution)/shard_map/dilated_attention/pallas_call | solution.py:515
  32.3 0.0 copy-done
  32.3 1.5 %projection.1 = bf16[512,768]{1,0:T(8,128)(2,1)} custom-call(bf16[512,768]{1,0:T(8,128)(2,1)S(1)} %dilated_attention.1.merged_ref, bf16[768,768]{1,0:T(8,128)(2,1)S(1)} %copy-done), custom_call_target="tpu_custom_call" | custom-call | tf_op jit(solution)/shard_map/projection/pallas_call | solution.py:525
Async XLA Ops:
  0.0 32.3 %copy-start = (bf16[768,768]{1,0:T(8,128)(2,1)S(1)}, bf16[768,768]{1,0:T(8,128)(2,1)}, u32[]{:S(2)}) copy-start(bf16[768,768]{1,0:T(8,128)(2,1)} %w_ref.1) | copy-start | bytes 3538948

commit v4 on v3

--- a/solution.py
+++ b/solution.py
@@ -107,10 +107,9 @@
     l2_sib = remote(8, 8, x2, c2.at[0, core], sibling)
     l2_pair = []
     for t in range(3):
-        tile = pl.ds(128 * t, 128)
         l2_pair += [
-            remote(9 + 2 * t, 9 + 2 * t, c2.at[0, core, :, :, tile], c2.at[1, core, :, :, tile], pair),
-            remote(10 + 2 * t, 10 + 2 * t, x2.at[:, :, tile], c2.at[1, core, :, :, tile], pair_other),
+            remote(9 + 2 * t, 9 + 2 * t, c2.at[0, core, t], c2.at[1, core, t], pair),
+            remote(10 + 2 * t, 10 + 2 * t, x2.at[t], c2.at[1, core, t], pair_other),
         ]
     l4_mirror = to_mirror(15, c4, x4)
     l3_mirror = to_mirror(17, c3, x3)
@@ -188,8 +187,11 @@
     stage[2] = permuted(q_ref, theirs)
     q_copy.start()
     for kind in range(2):
-        c2[0, core, kind] = select(halves.at[0, kind], mine_cols, 2)
-        x2[kind] = select(stage.at[kind], theirs_cols, 2)
+        own_rows = select(halves.at[0, kind], mine_cols, 2)
+        other_rows = select(stage.at[kind], theirs_cols, 2)
+        for t in range(3):
+            c2[0, core, t, kind] = own_rows[:, 128 * t:128 * t + 128]
+            x2[t, kind] = other_rows[:, 128 * t:128 * t + 128]
 
     @pl.when(is_centre)
     def _():
@@ -228,13 +230,12 @@
                 q = jnp.concatenate([jnp.where(m, q, jnp.zeros((), BF)) for m in masks], axis=0)
             return lax.dot_general(q, k, NT, preferred_element_type=F32)
 
-        following = scores(heads[0])
+        following = None
         for first in range(heads[0], heads[1], group):
             start, width = window(first, group)
             masks = [head_mask(first + g, start, width) for g in range(group)]
-            s = following
-            if first + group < heads[1]:
-                following = scores(first + group)
+            s = following if following is not None else scores(first)
+            following = scores(first + 1) if group == 1 and first + 1 < heads[1] else None
             o, top, total = softmax_unit(s, v_of(start, width))
             if norm:
                 o = o * (1.0 / total)
@@ -403,11 +404,16 @@
         acc0[src] = widened(share0) * acc0[src] + widened(share1) * full(acc1, 1, src)
 
     l2_sib.wait_recv()
+    def tiles2(kind):
+        return lambda a, w: jnp.concatenate([
+            jnp.concatenate([c2[slot, tok, t, kind] for t in range(a // 128, (a + w) // 128)], axis=1)
+            for slot in range(2) for tok in range(2)], axis=0)
+
     for tile in range(3):
         for c in l2_pair[2 * tile:2 * tile + 2]:
             c.wait_recv()
         attend(
-            lambda a, w: q2[:, a:a + w], chips(c2, 0, 2), chips(c2, 1, 2), 2, 2 * KEPT[2], acc2, top2, sum2,
+            lambda a, w: q2[:, a:a + w], tiles2(0), tiles2(1), 2, 2 * KEPT[2], acc2, top2, sum2,
             ((0, 2), (2, 4), (4, NH))[tile],
         )
 
@@ -490,8 +496,8 @@
     n = [2 * k for k in KEPT]
     bf = [
         (ROWS, WIDTH), (ROWS, WIDTH), (ROWS, WIDTH), (3, ROWS, HALF), (2, 3, ROWS, HALF), (2, n[1], HALF),
-        (2, 2, 2, KEPT[2], HALF), (4, 2, 2, KEPT[3], HALF), (4, 2, 2, KEPT[4], HALF),
-        (2, KEPT[2], HALF), (2, KEPT[3], HALF), (2, KEPT[4], HALF),
+        (2, 2, 3, 2, KEPT[2], 128), (4, 2, 2, KEPT[3], HALF), (4, 2, 2, KEPT[4], HALF),
+        (3, 2, KEPT[2], 128), (2, KEPT[3], HALF), (2, KEPT[4], HALF),
         (n[1], HALF), (n[2], HALF), (2 * n[3], HALF), (4, n[4], HALF),
     ]
     scratch = [pltpu.VMEM((5, 16), jnp.int32)] + [pltpu.VMEM(shape, BF) for shape in bf]

time: 34.1 us -> 34.4 us (level)
  no operation moved by 1% of the time
where the time goes in v4:
time: 34.4 us; the launch traced here: 34 us
  Pallas kernels  33.9 us (99%)
    pallas_call x1, Pallas kernels, body(): pl.pallas_call(kernel, out_shape=pltpu.VMEM((ROWS, WIDTH), BF), in_specs=...  32.3 us
    pallas_call x1, Pallas kernels, body(): pl.pallas_call(project, out_shape=jax.ShapeDtypeStruct((ROWS, WIDTH), BF)...  1.54 us

profile of v4, /device:TPU:1, one launch (start us, length us, event | category | flops | bytes accessed | tf_op | source)
XLA Modules:
  0.0 34.0 jit_solution(10112865071440467378)
XLA Ops:
  0.0 0.0 copy-start
  0.0 32.3 %dilated_attention.1.merged_ref = bf16[512,768]{1,0:T(8,128)(2,1)S(1)} custom-call(s32[5,16]{1,0:T(8,128)} %off_hbm.1, bf16[512,768]{1,0:T(8,128)(2,1)} %q_hbm.1, bf16[512,768]{1,0:T(8,128)(2,1)} %k_hbm.1, bf16[512,768]{1,0:T(8,128)(2,1)} %v_hbm.1), custom_call_target="tpu_custom_call" | custom-call | flops 3000000000 | bytes 5000000 | tf_op jit(solution)/shard_map/dilated_attention/pallas_call | solution.py:521
  32.3 0.0 copy-done
  32.3 1.5 %projection.1 = bf16[512,768]{1,0:T(8,128)(2,1)} custom-call(bf16[512,768]{1,0:T(8,128)(2,1)S(1)} %dilated_attention.1.merged_ref, bf16[768,768]{1,0:T(8,128)(2,1)S(1)} %copy-done), custom_call_target="tpu_custom_call" | custom-call | tf_op jit(solution)/shard_map/projection/pallas_call | solution.py:531
Async XLA Ops:
  0.0 32.3 %copy-start = (bf16[768,768]{1,0:T(8,128)(2,1)S(1)}, bf16[768,768]{1,0:T(8,128)(2,1)}, u32[]{:S(2)}) copy-start(bf16[768,768]{1,0:T(8,128)(2,1)} %w_ref.1) | copy-start | bytes 3538948
